TPU v7x, 256 devices: a whole 4x4x8 slice. The times are simulated.
256 devices in a mesh: wide: 16 (over x_hi, z), narrow: 16 (over x_lo, y, core).
Axes of the slice: x: 4 (x_hi: 2, x_lo: 2; x = x_hi * 2 + x_lo), y: 4, z: 8, core: 2. Of those that a mesh axis runs over, the one named last changes fastest.
Arguments:
- pair_act: bfloat16 [768, 768, 128], P('wide', 'narrow'), may hold values from -6 to 6
- residue_mask: int32 [768], replicated, may hold values 0 or 1
- w_proj_start: bfloat16 [128, 512], replicated, may hold values from -0.5 to 0.5
- w_bias_start: bfloat16 [128, 4], replicated, may hold values from -40 to 40
- w_out_start: bfloat16 [128, 128], replicated, may hold values from -0.5 to 0.5
- w_proj_end: bfloat16 [128, 512], replicated, may hold values from -0.5 to 0.5
- w_bias_end: bfloat16 [128, 4], replicated, may hold values from -40 to 40
- w_out_end: bfloat16 [128, 128], replicated, may hold values from -0.5 to 0.5
Outputs:
- update_start: bfloat16 [768, 768, 128], P('wide', 'narrow')
- update_end: bfloat16 [768, 768, 128], P('wide', 'narrow')
All inputs are finite; a program needn't handle non-finite values.
Results may differ from a plain program's by a relative error of at most 0.012.
The roundings to bfloat16 on the way count: a program that leaves them out, or rounds other values in their place, can miss the bound.
Values may be sent and summed in bfloat16 or wider, within the bound.
A program may use at most 64 MiB of HBM per device.

v0:
```python
import jax
import jax.numpy as jnp
from jax import lax
from jax.sharding import Mesh
from jax.sharding import PartitionSpec as P

NARROW = ("narrow_0", "narrow_1", "narrow_2")
norm_eps = 1e-05
masked_score = -1000000000.0


def cut_along(x, dim, count):
    before, after = (x.shape[:dim], x.shape[dim + 1 :])
    return jnp.moveaxis(x.reshape(*before, count, -1, *after), dim, 0)


def in_order(parts, dim):
    parts = jnp.moveaxis(parts, 0, dim)
    shape = parts.shape
    return parts.reshape(*shape[:dim], shape[dim] * shape[dim + 1], *shape[dim + 2 :])


def turned_blocks(parts, axes, order):
    inside = parts.shape[1:]
    out = parts.reshape(*(lax.axis_size(a) for a in axes), *inside)
    for k in order:
        out = lax.all_to_all(out, axes[k], k, k, tiled=True)
    return out.reshape(-1, *inside)


def two_step_exchange(x, groups, order, split_dim, concat_dim):
    count = lax.axis_size(groups[0]) * lax.axis_size(groups[1])
    parts = cut_along(x, split_dim, count)
    return in_order(turned_blocks(parts, groups, order), concat_dim)


def layer_norm(features):
    average = jnp.mean(features, axis=-1, keepdims=True)
    centred = features - average
    spread = jnp.mean(centred * centred, axis=-1, keepdims=True)
    return (centred * lax.rsqrt(spread + norm_eps)).astype(jnp.bfloat16)


def attend(projected, pair_bias, row_ok, key_ok, head_count, head_dim):
    length = projected.shape[1]
    inv_root = head_dim ** (-0.5)

    def one_row(item_pair):
        packed, valid_row = item_pair
        packed = packed.reshape(length, head_count, 4, head_dim)
        queries = packed[:, :, 0]
        keyset = packed[:, :, 1]
        values = packed[:, :, 2]
        gating = packed[:, :, 3]
        scores = (
            jnp.einsum("bhd,khd->hbk", queries, keyset, preferred_element_type=jnp.float32)
            * inv_root
            + pair_bias
        )
        allowed = jnp.logical_and(valid_row, key_ok)
        scores = jnp.where(allowed[None, None, :], scores, masked_score)
        weights = jax.nn.softmax(scores, axis=-1).astype(jnp.bfloat16)
        summed = jnp.einsum("hbk,khd->bhd", weights, values, preferred_element_type=jnp.float32)
        gated = (jax.nn.sigmoid(gating.astype(jnp.float32)) * summed).astype(jnp.bfloat16)
        return gated.reshape(length, head_count * head_dim)

    return lax.map(one_row, (projected, row_ok))


def on_device(
    pair_act,
    residue_mask,
    w_proj_start,
    w_bias_start,
    w_out_start,
    w_proj_end,
    w_bias_end,
    w_out_end,
):
    wide_count = lax.axis_size("wide")
    narrow_count = lax.axis_size(NARROW)
    wide_at = lax.axis_index("wide")
    narrow_at = lax.axis_index(NARROW)
    tile_rows, tile_cols, channels = pair_act.shape
    head_count = w_bias_start.shape[1]
    head_dim = w_out_start.shape[0] // head_count
    residue_ok = residue_mask > 0
    normed = layer_norm(pair_act.astype(jnp.float32))
    groups = narrow_count // head_count
    sub_rows = tile_rows // groups
    proj_tile = jnp.einsum(
        "ijc,chx->hijx",
        normed,
        w_proj_start.reshape(channels, head_count, -1),
        preferred_element_type=jnp.float32,
    ).astype(jnp.bfloat16)
    outgoing = proj_tile.reshape(narrow_count, sub_rows, tile_cols, -1)
    bias_tile = jnp.einsum("ijc,ch->hij", normed, w_bias_start, preferred_element_type=jnp.float32)
    bias_out = jnp.repeat(bias_tile, groups, axis=0)
    incoming = two_step_exchange(outgoing, (("narrow_0", "narrow_1"), "narrow_2"), (1, 0), 0, 2)
    bias_rows = lax.all_to_all(bias_out, NARROW, split_axis=0, concat_axis=2, tiled=True)
    pair_bias = lax.all_gather(bias_rows, "wide", axis=1, tiled=True)
    group_at = narrow_at % groups
    first_row = wide_at * tile_rows + group_at * sub_rows
    row_ok = lax.dynamic_slice_in_dim(residue_ok, first_row, sub_rows)
    gated = attend(incoming[0], pair_bias, row_ok, residue_ok, 1, head_dim)
    returned = lax.all_to_all(
        gated.reshape(sub_rows, -1), NARROW, split_axis=1, concat_axis=0, tiled=True
    )
    head_tile = returned.reshape(head_count, tile_rows, tile_cols, head_dim)
    update_start = jnp.einsum(
        "hijd,hdc->ijc",
        head_tile,
        w_out_start.reshape(head_count, head_dim, channels),
        preferred_element_type=jnp.float32,
    ).astype(jnp.bfloat16)
    updated = pair_act.astype(jnp.float32) + update_start.astype(jnp.float32)
    normed_end = layer_norm(updated)
    groups_wide = wide_count // head_count
    sub_cols = tile_cols // groups_wide
    proj_end_tile = jnp.einsum(
        "ijc,chx->hjix",
        normed_end,
        w_proj_end.reshape(channels, head_count, -1),
        preferred_element_type=jnp.float32,
    ).astype(jnp.bfloat16)
    outgoing_end = proj_end_tile.reshape(wide_count, sub_cols, tile_rows, -1)
    bias_end_tile = jnp.einsum(
        "ijc,ch->hji", normed_end, w_bias_end, preferred_element_type=jnp.float32
    )
    bias_end_out = jnp.repeat(bias_end_tile, groups_wide, axis=0)
    incoming_end = lax.all_to_all(outgoing_end, "wide", split_axis=0, concat_axis=2, tiled=True)
    bias_cols = lax.all_to_all(bias_end_out, "wide", split_axis=0, concat_axis=2, tiled=True)
    pair_bias_end = lax.all_gather(bias_cols, NARROW, axis=1, tiled=True)
    group_wide = wide_at % groups_wide
    first_col = narrow_at * tile_cols + group_wide * sub_cols
    col_ok = lax.dynamic_slice_in_dim(residue_ok, first_col, sub_cols)
    gated_end = attend(incoming_end[0], pair_bias_end, col_ok, residue_ok, 1, head_dim)
    returned_end = lax.all_to_all(
        gated_end.reshape(sub_cols, -1), "wide", split_axis=1, concat_axis=0, tiled=True
    )
    head_tile_end = returned_end.reshape(head_count, tile_cols, tile_rows, head_dim)
    update_end = jnp.einsum(
        "hjid,hdc->ijc",
        head_tile_end,
        w_out_end.reshape(head_count, head_dim, channels),
        preferred_element_type=jnp.float32,
    ).astype(jnp.bfloat16)
    return (update_start, update_end)


def solution(mesh):
    split = Mesh(
        mesh.devices.reshape(mesh.shape["wide"], 2, 4, 2),
        ("wide", "narrow_0", "narrow_1", "narrow_2"),
    )
    placed = (P("wide", NARROW, None), P(), P(), P(), P(), P(), P(), P())
    return jax.shard_map(
        on_device,
        mesh=split,
        in_specs=placed,
        out_specs=(P("wide", NARROW, None), P("wide", NARROW, None)),
        check_vma=False,
    )
```

profile of v0, /device:TPU:40, one launch (start us, length us, event | category | flops | bytes accessed | tf_op | source)
XLA Modules:
  0.0 379.8 jit_solution(18101503657099255865)
XLA Ops:
  7.2 1.5 convert_reduce_fusion
  8.7 1.8 fusion.21
  10.5 1.9 convolution_bitcast_fusion.3
  12.9 10.5 %all_to_all.95 = f32[16,1,2304]{2,1,0:T(1,128)S(1)} all-to-all(f32[16,1,2304]{2,1,0:T(1,128)S(1)} %reshape.255), channel_id=1, replica_groups=mesh['wide'=16,'narrow_0'=2,'narrow_1'=4,'narrow_2'=2] {'narrow_0','narr..., dimensions={0} | all-to-all | bytes 294912 | tf_op jit(solution)/shard_map/all_to_all | solution.py:101
  25.3 1.0 all_to_all.86
  26.4 1.1 convert_bitcast_fusion.1
  28.3 5.6 %all_to_all.96 = bf16[8,2,1,12,48,128]{5,4,3,0,2,1:T(8,128)(2,1)S(1)} all-to-all(bf16[8,2,1,12,48,128]{5,4,3,0,2,1:T(8,128)(2,1)S(1)} %copy.76), channel_id=1, replica_groups=mesh['wide'=16,'narrow_0'=2,'narrow_1'=4,'narrow_2'=2] {'narrow_2'}, dimensions={1} | all-to-all | bytes 4718592 | tf_op jit(solution)/shard_map/all_to_all | solution.py:27
  33.9 1.8 copy.77
  35.7 5.8 %all-to-all-start.1 = ((bf16[8,2,1,12,48,128]{5,4,3,1,2,0:T(8,128)(2,1)}), bf16[8,2,1,12,48,128]{5,4,3,1,2,0:T(8,128)(2,1)S(1)}, u32[]{:S(2)}, u32[]{:S(2)}) async-start(bf16[8,2,1,12,48,128]{5,4,3,1,2,0:T(8,128)(2,1)} %copy.77), calls=%async_computation.1 | async-start | bytes 4718592 | tf_op jit(solution)/shard_map/all_to_all | solution.py:27
  41.6 28.6 %all-to-all-done.1 = bf16[8,2,1,12,48,128]{5,4,3,1,2,0:T(8,128)(2,1)S(1)} async-done(((bf16[8,2,1,12,48,128]{5,4,3,1,2,0:T(8,128)(2,1)}), bf16[8,2,1,12,48,128]{5,4,3,1,2,0:T(8,128)(2,1)S(1)}, u32[]{:S(2)}, u32[]{:S(2)}) %all-to-all-start.1) | async-done | bytes 2359328 | tf_op jit(solution)/shard_map/all_to_all | solution.py:27
  70.2 2.0 copy.78
  72.2 43.2 %all-gather.3.cloned.1.call-done = f32[1,768,768]{2,0,1:T(1,128)} async-done(((f32[1,48,768]{2,0,1:T(1,128)}), f32[1,768,768]{2,0,1:T(1,128)}) %all-gather.3.cloned.1.call-update) | async-done | bytes 2359312 | tf_op jit(solution)/shard_map/all_gather | solution.py:102
  115.4 5.5 %copy.83 = f32[1,768,768]{1,2,0:T(8,128)S(1)} copy(f32[1,768,768]{2,0,1:T(1,128)} %all-gather.3.cloned.1.call-done) | data formatting | bytes 4718592 | tf_op jit(solution)/shard_map/while | solution.py:67
  121.8 52.3 %while.20 = (s32[]{:T(128)}, bf16[12,768,32]{1,2,0:T(8,128)(2,1)}, bf16[12,768,128]{2,1,0:T(8,128)(2,1)}, pred[12]{0:T(512)(128)(4,1)S(1)}, pred[768]{0:T(1024)(...) while((s32[]{:T(128)}, bf16[12,768,32]{1,2,0:T(8,128)(2,1)}, bf16[12,768,128]{2,1,0:T(8,128)(2,1)}, ...), condition=%wide.region_5.6_spmd, body=%wide.region_2.5_spmd.sunk | while | flops 80952576 | bytes 10489944 | solution.py:67
  125.0 1.1 fusion.50
  129.3 1.1 fusion.50
  133.7 1.1 fusion.50
  138.1 1.1 fusion.50
  142.4 1.1 fusion.50
  146.8 1.1 fusion.50
  151.1 1.1 fusion.50
  155.5 1.1 fusion.50
  159.9 1.1 fusion.50
  164.2 1.1 fusion.50
  168.6 1.1 fusion.50
  172.9 1.1 fusion.50
  174.1 2.0 copy.84
  176.1 3.0 all_to_all.73
  179.2 1.4 copy.85
  180.6 15.9 %all_to_all.97 = bf16[12,16,1536]{2,0,1:T(8,128)(2,1)} all-to-all(bf16[12,16,1536]{2,0,1:T(8,128)(2,1)S(1)} %copy.85), channel_id=1, replica_groups=mesh['wide'=16,'narrow_0'=2,'narrow_1'=4,'narrow_2'=2] {'narrow_0','narr..., dimensions={1} | all-to-all | bytes 1179648 | tf_op jit(solution)/shard_map/all_to_all | solution.py:107
  196.5 3.0 reshape.234
  199.5 1.4 fusion.24
  202.9 1.0 reshape.257
  203.9 6.7 %all-to-all-start.5 = ((f32[16,1,2304]{2,1,0:T(1,128)}), f32[16,1,2304]{2,1,0:T(1,128)S(1)}, u32[]{:S(2)}, u32[]{:S(2)}) async-start(f32[16,1,2304]{2,1,0:T(1,128)} %reshape.257), calls=%async_computation.5 | async-start | bytes 294912 | tf_op jit(solution)/shard_map/all_to_all | solution.py:133
  210.6 1.9 convert_bitcast_fusion
  212.5 2.9 copy.88
  215.5 5.7 %all-to-all-done.5 = f32[16,1,2304]{2,1,0:T(1,128)S(1)} async-done(((f32[16,1,2304]{2,1,0:T(1,128)}), f32[16,1,2304]{2,1,0:T(1,128)S(1)}, u32[]{:S(2)}, u32[]{:S(2)}) %all-to-all-start.5) | async-done | bytes 147488 | tf_op jit(solution)/shard_map/all_to_all | solution.py:133
  221.2 4.0 %all-to-all-start.4 = ((bf16[16,12,48,128]{3,2,1,0:T(8,128)(2,1)}), bf16[16,12,48,128]{3,2,1,0:T(8,128)(2,1)S(1)}, u32[]{:S(2)}, u32[]{:S(2)}) async-start(bf16[16,12,48,128]{3,2,1,0:T(8,128)(2,1)} %bitcast.42), calls=%async_computation.4 | async-start | bytes 4718592 | tf_op jit(solution)/shard_map/all_to_all | solution.py:132
  226.8 1.0 all_to_all.87
  227.9 52.0 %all-to-all-done.4 = bf16[16,12,48,128]{3,2,1,0:T(8,128)(2,1)S(1)} async-done(((bf16[16,12,48,128]{3,2,1,0:T(8,128)(2,1)}), bf16[16,12,48,128]{3,2,1,0:T(8,128)(2,1)S(1)}, u32[]{:S(2)}, u32[]{:S(2)}) %all-to-all-start.4) | async-done | bytes 2359328 | tf_op jit(solution)/shard_map/all_to_all | solution.py:132
  279.9 2.0 copy.89
  281.9 5.5 %copy.94 = f32[1,768,768]{1,2,0:T(8,128)S(1)} copy(f32[1,768,768]{2,0,1:T(1,128)} %all-gather.5.cloned.1.call-done) | data formatting | bytes 4718592 | tf_op jit(solution)/shard_map/while | solution.py:67
  287.4 46.0 %while.21 = (s32[]{:T(128)}, bf16[12,768,32]{1,2,0:T(8,128)(2,1)S(1)}, bf16[12,768,128]{2,1,0:T(8,128)(2,1)}, pred[12]{0:T(512)(128)(4,1)S(1)}, pred[768]{0:T(10...) while((s32[]{:T(128)}, bf16[12,768,32]{1,2,0:T(8,128)(2,1)S(1)}, ...), condition=%wide.region_11.12_spmd, body=%wide.region_8.11_spmd.sunk | while | flops 80952576 | bytes 10489436 | solution.py:67
  333.5 1.1 copy.95
  334.6 2.3 all_to_all.83
  337.3 32.0 %all_to_all.98 = bf16[12,16,1536]{2,0,1:T(8,128)(2,1)S(1)} all-to-all(bf16[12,16,1536]{2,0,1:T(8,128)(2,1)S(1)} %copy.96), channel_id=1, replica_groups=mesh['wide'=16,'narrow_0'=2,'narrow_1'=4,'narrow_2'=2] {'wide'}, dimensions={1} | all-to-all | bytes 1179648 | tf_op jit(solution)/shard_map/all_to_all | solution.py:139
  369.3 1.6 reshape.239
  370.9 1.1 fusion.20
  (203 shorter events, 93.2 us)
Async XLA Ops:
  7.2 19.2 %copy-start = (bf16[128,512]{1,0:T(8,128)(2,1)S(1)}, bf16[128,512]{1,0:T(8,128)(2,1)}, u32[]{:S(2)}) copy-start(bf16[128,512]{1,0:T(8,128)(2,1)} %param.14) | copy-start | bytes 393220
  7.2 108.2 %all-gather.3.cloned.1.call-start = ((), (), s32[]{:S(2)}) async-start(), calls=%async_computation.7 | async-start | bytes 2506752 | tf_op jit(solution)/shard_map/all_gather | solution.py:102
  10.5 15.9 %copy-start.1 = (bf16[48,48,128]{2,1,0:T(8,128)(2,1)S(1)}, bf16[48,48,128]{2,1,0:T(8,128)(2,1)}, u32[]{:S(2)}) copy-start(bf16[48,48,128]{2,1,0:T(8,128)(2,1)} %param.12) | copy-start | bytes 1769476
  35.7 5.8 %copy-start.6 = (s32[768]{0:T(1024)S(1)}, s32[768]{0:T(1024)}, u32[]{:S(2)}) copy-start(s32[768]{0:T(1024)} %param.13) | copy-start | bytes 9220
  35.7 34.5 %all-to-all-start.1 = ((bf16[8,2,1,12,48,128]{5,4,3,1,2,0:T(8,128)(2,1)}), bf16[8,2,1,12,48,128]{5,4,3,1,2,0:T(8,128)(2,1)S(1)}, u32[]{:S(2)}, u32[]{:S(2)}) async-start(bf16[8,2,1,12,48,128]{5,4,3,1,2,0:T(8,128)(2,1)} %copy.77), calls=%async_computation.1 | async-start | bytes 4718592 | tf_op jit(solution)/shard_map/all_to_all | solution.py:27
  180.6 18.9 %copy-start.4 = (bf16[128,128]{1,0:T(8,128)(2,1)S(1)}, bf16[128,128]{1,0:T(8,128)(2,1)}, u32[]{:S(2)}) copy-start(bf16[128,128]{1,0:T(8,128)(2,1)} %param.16) | copy-start | bytes 98308
  199.4 2.3 copy-start.7
  200.9 0.8 copy-start.2
  200.9 9.7 %copy-start.3 = (bf16[128,512]{1,0:T(8,128)(2,1)S(1)}, bf16[128,512]{1,0:T(8,128)(2,1)}, u32[]{:S(2)}) copy-start(bf16[128,512]{1,0:T(8,128)(2,1)} %param.17) | copy-start | bytes 393220
  203.9 17.3 %all-to-all-start.5 = ((f32[16,1,2304]{2,1,0:T(1,128)}), f32[16,1,2304]{2,1,0:T(1,128)S(1)}, u32[]{:S(2)}, u32[]{:S(2)}) async-start(f32[16,1,2304]{2,1,0:T(1,128)} %reshape.257), calls=%async_computation.5 | async-start | bytes 294912 | tf_op jit(solution)/shard_map/all_to_all | solution.py:133
  221.2 58.7 %all-to-all-start.4 = ((bf16[16,12,48,128]{3,2,1,0:T(8,128)(2,1)}), bf16[16,12,48,128]{3,2,1,0:T(8,128)(2,1)S(1)}, u32[]{:S(2)}, u32[]{:S(2)}) async-start(bf16[16,12,48,128]{3,2,1,0:T(8,128)(2,1)} %bitcast.42), calls=%async_computation.4 | async-start | bytes 4718592 | tf_op jit(solution)/shard_map/all_to_all | solution.py:132
  225.2 56.7 %all-gather.5.cloned.1.call-start = ((), (), s32[]{:S(2)}) async-start(), calls=%async_computation.8 | async-start | bytes 2506752 | tf_op jit(solution)/shard_map/all_gather | solution.py:134
  337.3 33.6 %copy-start.5 = (bf16[128,128]{1,0:T(8,128)(2,1)S(1)}, bf16[128,128]{1,0:T(8,128)(2,1)}, u32[]{:S(2)}) copy-start(bf16[128,128]{1,0:T(8,128)(2,1)} %param.19) | copy-start | bytes 98308
Sparse Core Ops, SparseCore 0:
  26.5 88.9 all-gather.2
  228.5 46.1 all-gather.4
where the time goes:
time: 382 us; the launch traced here: 380 us
  waiting for transfers between devices  130 us (34%)
  local copies, waits for them, and re-layouts  82.4 us (22%)
  blocking collectives  64 us (17%)
  matrix products  42.6 us (11%)
  other arithmetic  29.4 us (8%)
  starting transfers between devices  16.8 us (4%)
  between operations  14.4 us (4%)
    all_to_all x1, waiting for transfers between devices, on_device(): lax.all_to_all(outgoing_end, 'wide', split_axis=0, concat_axis=2, tiled=T...  52 us
    all_gather x1, waiting for transfers between devices, on_device(): pair_bias = lax.all_gather(bias_rows, 'wide', axis=1, tiled=True)  43.2 us
    dynamic_slice x72, local copies, waits for them, and re-layouts, attend(): return lax.map(one_row, (projected, row_ok))  40.2 us
    all_to_all x1, blocking collectives, on_device(): lax.all_to_all(gated_end.reshape(sub_cols, -1), 'wide', split_axis=1, con...  32 us
    all_to_all x1, waiting for transfers between devices, turned_blocks(): out = lax.all_to_all(out, axes[k], k, k, tiled=True)  28.6 us
    dot_general x24, matrix products, one_row(): jnp.einsum('hbk,khd->bhd', weights, values, preferred_element_type=jnp.fl...  19.8 us
    all_to_all x1, blocking collectives, on_device(): lax.all_to_all(gated.reshape(sub_rows, -1), NARROW, split_axis=1, concat_...  15.9 us
    and x24, other arithmetic, one_row(): allowed = jnp.logical_and(valid_row, key_ok)  14.6 us
  transfers between devices with their start and end apart: 5, of which 4 were waited for; matrix products, arithmetic and copies ran while one was open for 4% of the time, Pallas kernels for 0%

commit v1 on v0

--- a/solution.py
+++ b/solution.py
@@ -136,8 +136,12 @@
     first_col = narrow_at * tile_cols + group_wide * sub_cols
     col_ok = lax.dynamic_slice_in_dim(residue_ok, first_col, sub_cols)
     gated_end = attend(incoming_end[0], pair_bias_end, col_ok, residue_ok, 1, head_dim)
-    returned_end = lax.all_to_all(
-        gated_end.reshape(sub_cols, -1), "wide", split_axis=1, concat_axis=0, tiled=True
+    xin = gated_end.reshape(sub_cols, -1)
+    returned_end = jnp.concatenate(
+        lax.all_to_all(
+            jnp.stack(jnp.split(xin, lax.axis_size("wide"), axis=1), axis=0), "wide", 0, 0
+        ),
+        axis=0,
     )
     head_tile_end = returned_end.reshape(head_count, tile_cols, tile_rows, head_dim)
     update_end = jnp.einsum(

time: 382 us -> 382 us (level)
  no operation moved by 1% of the time
where the time goes in v1:
time: 382 us; the launch traced here: 380 us
  waiting for transfers between devices  130 us (34%)
  local copies, waits for them, and re-layouts  82.3 us (22%)
  blocking collectives  64 us (17%)
  matrix products  42.6 us (11%)
  other arithmetic  29.4 us (8%)
  starting transfers between devices  16.8 us (4%)
  between operations  14.5 us (4%)
    all_to_all x1, waiting for transfers between devices, on_device(): lax.all_to_all(outgoing_end, 'wide', split_axis=0, concat_axis=2, tiled=T...  52 us
    all_gather x1, waiting for transfers between devices, on_device(): pair_bias = lax.all_gather(bias_rows, 'wide', axis=1, tiled=True)  43.2 us
    dynamic_slice x72, local copies, waits for them, and re-layouts, attend(): return lax.map(one_row, (projected, row_ok))  40.2 us
    all_to_all x1, blocking collectives, on_device(): lax.all_to_all(jnp.stack(jnp.split(xin, lax.axis_size('wide'), axis=1), a...  32 us
    all_to_all x1, waiting for transfers between devices, turned_blocks(): out = lax.all_to_all(out, axes[k], k, k, tiled=True)  28.6 us
    dot_general x24, matrix products, one_row(): jnp.einsum('hbk,khd->bhd', weights, values, preferred_element_type=jnp.fl...  19.8 us
    all_to_all x1, blocking collectives, on_device(): lax.all_to_all(gated.reshape(sub_rows, -1), NARROW, split_axis=1, concat_...  15.9 us
    and x24, other arithmetic, one_row(): allowed = jnp.logical_and(valid_row, key_ok)  14.6 us
  transfers between devices with their start and end apart: 5, of which 4 were waited for; matrix products, arithmetic and copies ran while one was open for 4% of the time, Pallas kernels for 0%

profile of v1, /device:TPU:40, one launch (start us, length us, event | category | flops | bytes accessed | tf_op | source)
XLA Modules:
  0.0 379.8 jit_solution(4201115804198996365)
XLA Ops:
  7.2 1.5 convert_reduce_fusion
  8.7 1.8 fusion.21
  10.5 1.9 convolution_bitcast_fusion.3
  12.9 10.5 %all_to_all.84 = f32[16,1,2304]{2,1,0:T(1,128)S(1)} all-to-all(f32[16,1,2304]{2,1,0:T(1,128)S(1)} %reshape.249), channel_id=1, replica_groups=mesh['wide'=16,'narrow_0'=2,'narrow_1'=4,'narrow_2'=2] {'narrow_0','narr..., dimensions={0} | all-to-all | bytes 294912 | tf_op jit(solution)/shard_map/all_to_all | solution.py:101
  25.3 1.0 all_to_all.75
  26.4 1.1 convert_bitcast_fusion.1
  28.3 5.6 %all_to_all.85 = bf16[8,2,1,12,48,128]{5,4,3,0,2,1:T(8,128)(2,1)S(1)} all-to-all(bf16[8,2,1,12,48,128]{5,4,3,0,2,1:T(8,128)(2,1)S(1)} %copy.73), channel_id=1, replica_groups=mesh['wide'=16,'narrow_0'=2,'narrow_1'=4,'narrow_2'=2] {'narrow_2'}, dimensions={1} | all-to-all | bytes 4718592 | tf_op jit(solution)/shard_map/all_to_all | solution.py:27
  33.9 1.8 copy.74
  35.7 5.8 %all-to-all-start.1 = ((bf16[8,2,1,12,48,128]{5,4,3,1,2,0:T(8,128)(2,1)}), bf16[8,2,1,12,48,128]{5,4,3,1,2,0:T(8,128)(2,1)S(1)}, u32[]{:S(2)}, u32[]{:S(2)}) async-start(bf16[8,2,1,12,48,128]{5,4,3,1,2,0:T(8,128)(2,1)} %copy.74), calls=%async_computation.1 | async-start | bytes 4718592 | tf_op jit(solution)/shard_map/all_to_all | solution.py:27
  41.6 28.6 %all-to-all-done.1 = bf16[8,2,1,12,48,128]{5,4,3,1,2,0:T(8,128)(2,1)S(1)} async-done(((bf16[8,2,1,12,48,128]{5,4,3,1,2,0:T(8,128)(2,1)}), bf16[8,2,1,12,48,128]{5,4,3,1,2,0:T(8,128)(2,1)S(1)}, u32[]{:S(2)}, u32[]{:S(2)}) %all-to-all-start.1) | async-done | bytes 2359328 | tf_op jit(solution)/shard_map/all_to_all | solution.py:27
  70.2 2.0 copy.75
  72.2 43.2 %all-gather.3.cloned.1.call-done = f32[1,768,768]{2,0,1:T(1,128)} async-done(((f32[1,48,768]{2,0,1:T(1,128)}), f32[1,768,768]{2,0,1:T(1,128)}) %all-gather.3.cloned.1.call-update) | async-done | bytes 2359312 | tf_op jit(solution)/shard_map/all_gather | solution.py:102
  115.4 5.5 %copy.80 = f32[1,768,768]{1,2,0:T(8,128)S(1)} copy(f32[1,768,768]{2,0,1:T(1,128)} %all-gather.3.cloned.1.call-done) | data formatting | bytes 4718592 | tf_op jit(solution)/shard_map/while | solution.py:67
  121.8 52.3 %while.20 = (s32[]{:T(128)}, bf16[12,768,32]{1,2,0:T(8,128)(2,1)}, bf16[12,768,128]{2,1,0:T(8,128)(2,1)}, pred[12]{0:T(512)(128)(4,1)S(1)}, pred[768]{0:T(1024)(...) while((s32[]{:T(128)}, bf16[12,768,32]{1,2,0:T(8,128)(2,1)}, bf16[12,768,128]{2,1,0:T(8,128)(2,1)}, ...), condition=%wide.region_5.6_spmd, body=%wide.region_2.5_spmd.sunk | while | flops 80952576 | bytes 10489944 | solution.py:67
  125.0 1.1 fusion.66
  129.3 1.1 fusion.66
  133.7 1.1 fusion.66
  138.1 1.1 fusion.66
  142.4 1.1 fusion.66
  146.8 1.1 fusion.66
  151.1 1.1 fusion.66
  155.5 1.1 fusion.66
  159.9 1.1 fusion.66
  164.2 1.1 fusion.66
  168.6 1.1 fusion.66
  172.9 1.1 fusion.66
  174.1 2.0 copy.81
  176.1 3.0 all_to_all.64
  179.2 1.4 copy.82
  180.6 15.9 %all_to_all.86 = bf16[12,16,1536]{2,0,1:T(8,128)(2,1)} all-to-all(bf16[12,16,1536]{2,0,1:T(8,128)(2,1)S(1)} %copy.82), channel_id=1, replica_groups=mesh['wide'=16,'narrow_0'=2,'narrow_1'=4,'narrow_2'=2] {'narrow_0','narr..., dimensions={1} | all-to-all | bytes 1179648 | tf_op jit(solution)/shard_map/all_to_all | solution.py:107
  196.5 3.0 reshape.228
  199.5 1.4 fusion.24
  202.9 1.0 reshape.251
  203.9 6.7 %all-to-all-start.5 = ((f32[16,1,2304]{2,1,0:T(1,128)}), f32[16,1,2304]{2,1,0:T(1,128)S(1)}, u32[]{:S(2)}, u32[]{:S(2)}) async-start(f32[16,1,2304]{2,1,0:T(1,128)} %reshape.251), calls=%async_computation.5 | async-start | bytes 294912 | tf_op jit(solution)/shard_map/all_to_all | solution.py:133
  210.6 1.9 convert_bitcast_fusion
  212.5 2.9 copy.85
  215.5 5.7 %all-to-all-done.5 = f32[16,1,2304]{2,1,0:T(1,128)S(1)} async-done(((f32[16,1,2304]{2,1,0:T(1,128)}), f32[16,1,2304]{2,1,0:T(1,128)S(1)}, u32[]{:S(2)}, u32[]{:S(2)}) %all-to-all-start.5) | async-done | bytes 147488 | tf_op jit(solution)/shard_map/all_to_all | solution.py:133
  221.2 4.0 %all-to-all-start.4 = ((bf16[16,12,48,128]{3,2,1,0:T(8,128)(2,1)}), bf16[16,12,48,128]{3,2,1,0:T(8,128)(2,1)S(1)}, u32[]{:S(2)}, u32[]{:S(2)}) async-start(bf16[16,12,48,128]{3,2,1,0:T(8,128)(2,1)} %bitcast.42), calls=%async_computation.4 | async-start | bytes 4718592 | tf_op jit(solution)/shard_map/all_to_all | solution.py:132
  226.8 1.0 all_to_all.76
  227.9 52.0 %all-to-all-done.4 = bf16[16,12,48,128]{3,2,1,0:T(8,128)(2,1)S(1)} async-done(((bf16[16,12,48,128]{3,2,1,0:T(8,128)(2,1)}), bf16[16,12,48,128]{3,2,1,0:T(8,128)(2,1)S(1)}, u32[]{:S(2)}, u32[]{:S(2)}) %all-to-all-start.4) | async-done | bytes 2359328 | tf_op jit(solution)/shard_map/all_to_all | solution.py:132
  279.9 2.0 copy.86
  281.9 5.5 %copy.91 = f32[1,768,768]{1,2,0:T(8,128)S(1)} copy(f32[1,768,768]{2,0,1:T(1,128)} %all-gather.5.cloned.1.call-done) | data formatting | bytes 4718592 | tf_op jit(solution)/shard_map/while | solution.py:67
  287.4 46.0 %while.21 = (s32[]{:T(128)}, bf16[12,768,32]{1,2,0:T(8,128)(2,1)S(1)}, bf16[12,768,128]{2,1,0:T(8,128)(2,1)}, pred[12]{0:T(512)(128)(4,1)S(1)}, pred[768]{0:T(10...) while((s32[]{:T(128)}, bf16[12,768,32]{1,2,0:T(8,128)(2,1)S(1)}, ...), condition=%wide.region_11.12_spmd, body=%wide.region_8.11_spmd.sunk | while | flops 80952576 | bytes 10489436 | solution.py:67
  333.5 1.1 copy.92
  334.6 2.4 reshape.233
  337.3 32.0 %all_to_all.87 = bf16[16,12,1536]{2,1,0:T(8,128)(2,1)S(1)} all-to-all(bf16[16,12,1536]{2,1,0:T(8,128)(2,1)S(1)} %fusion.31), channel_id=1, replica_groups=mesh['wide'=16,'narrow_0'=2,'narrow_1'=4,'narrow_2'=2] {'wide'}, dimensions={0} | all-to-all | bytes 1179648 | tf_op jit(solution)/shard_map/all_to_all | solution.py:141
  369.3 1.6 reshape_reshape.3
  370.9 1.1 fusion.20
  (218 shorter events, 93.0 us)
Async XLA Ops:
  7.2 19.2 %copy-start = (bf16[128,512]{1,0:T(8,128)(2,1)S(1)}, bf16[128,512]{1,0:T(8,128)(2,1)}, u32[]{:S(2)}) copy-start(bf16[128,512]{1,0:T(8,128)(2,1)} %param.14) | copy-start | bytes 393220
  7.2 108.2 %all-gather.3.cloned.1.call-start = ((), (), s32[]{:S(2)}) async-start(), calls=%async_computation.7 | async-start | bytes 2506752 | tf_op jit(solution)/shard_map/all_gather | solution.py:102
  10.5 15.9 %copy-start.1 = (bf16[48,48,128]{2,1,0:T(8,128)(2,1)S(1)}, bf16[48,48,128]{2,1,0:T(8,128)(2,1)}, u32[]{:S(2)}) copy-start(bf16[48,48,128]{2,1,0:T(8,128)(2,1)} %param.12) | copy-start | bytes 1769476
  35.7 5.8 %copy-start.6 = (s32[768]{0:T(1024)S(1)}, s32[768]{0:T(1024)}, u32[]{:S(2)}) copy-start(s32[768]{0:T(1024)} %param.13) | copy-start | bytes 9220
  35.7 34.5 %all-to-all-start.1 = ((bf16[8,2,1,12,48,128]{5,4,3,1,2,0:T(8,128)(2,1)}), bf16[8,2,1,12,48,128]{5,4,3,1,2,0:T(8,128)(2,1)S(1)}, u32[]{:S(2)}, u32[]{:S(2)}) async-start(bf16[8,2,1,12,48,128]{5,4,3,1,2,0:T(8,128)(2,1)} %copy.74), calls=%async_computation.1 | async-start | bytes 4718592 | tf_op jit(solution)/shard_map/all_to_all | solution.py:27
  180.6 18.9 %copy-start.4 = (bf16[128,128]{1,0:T(8,128)(2,1)S(1)}, bf16[128,128]{1,0:T(8,128)(2,1)}, u32[]{:S(2)}) copy-start(bf16[128,128]{1,0:T(8,128)(2,1)} %param.16) | copy-start | bytes 98308
  199.4 2.3 copy-start.7
  200.9 0.8 copy-start.2
  200.9 9.7 %copy-start.3 = (bf16[128,512]{1,0:T(8,128)(2,1)S(1)}, bf16[128,512]{1,0:T(8,128)(2,1)}, u32[]{:S(2)}) copy-start(bf16[128,512]{1,0:T(8,128)(2,1)} %param.17) | copy-start | bytes 393220
  203.9 17.3 %all-to-all-start.5 = ((f32[16,1,2304]{2,1,0:T(1,128)}), f32[16,1,2304]{2,1,0:T(1,128)S(1)}, u32[]{:S(2)}, u32[]{:S(2)}) async-start(f32[16,1,2304]{2,1,0:T(1,128)} %reshape.251), calls=%async_computation.5 | async-start | bytes 294912 | tf_op jit(solution)/shard_map/all_to_all | solution.py:133
  221.2 58.7 %all-to-all-start.4 = ((bf16[16,12,48,128]{3,2,1,0:T(8,128)(2,1)}), bf16[16,12,48,128]{3,2,1,0:T(8,128)(2,1)S(1)}, u32[]{:S(2)}, u32[]{:S(2)}) async-start(bf16[16,12,48,128]{3,2,1,0:T(8,128)(2,1)} %bitcast.42), calls=%async_computation.4 | async-start | bytes 4718592 | tf_op jit(solution)/shard_map/all_to_all | solution.py:132
  225.2 56.7 %all-gather.5.cloned.1.call-start = ((), (), s32[]{:S(2)}) async-start(), calls=%async_computation.8 | async-start | bytes 2506752 | tf_op jit(solution)/shard_map/all_gather | solution.py:134
  337.3 33.6 %copy-start.5 = (bf16[128,128]{1,0:T(8,128)(2,1)S(1)}, bf16[128,128]{1,0:T(8,128)(2,1)}, u32[]{:S(2)}) copy-start(bf16[128,128]{1,0:T(8,128)(2,1)} %param.19) | copy-start | bytes 98308
Sparse Core Ops, SparseCore 0:
  26.5 88.9 all-gather.2
  228.5 46.1 all-gather.4
